TPU v7x, 32 devices: a whole 2x2x4 slice. The times are simulated.
32 devices in a mesh: fsdp: 4 (over y, x), ctx: 2 (over core), tp: 4 (over z).
Axes of the slice: x: 2, y: 2, z: 4, core: 2. Of those that a mesh axis runs over, the one named last changes fastest.
Arguments:
- inputs: float32 [2048, 2048], P(('fsdp', 'ctx')), may hold values from -6 to 6
- cotangent: float32 [2048, 2048], P(('fsdp', 'ctx')), may hold values from -6 to 6
- seq_lengths: int32 [4, 4], P('fsdp'), may hold values from 0 to 512, as said below
- slots: int32 [2048], P(('fsdp', 'ctx')), may hold values from 0 to 2047, as said below
- gain_in: float32 [2048], replicated, may hold values from 0.5 to 1.5
- w_z: float32 [2048, 4096], P(('fsdp', 'ctx'), 'tp'), may hold values from -0.125 to 0.125
- w_x: float32 [2048, 4096], P(('fsdp', 'ctx'), 'tp'), may hold values from -0.125 to 0.125
- w_dt: float32 [2048, 64], P(('fsdp', 'ctx'), 'tp'), may hold values from -0.125 to 0.125
- w_bc: float32 [2048, 256], P(('fsdp', 'ctx')), may hold values from -0.125 to 0.125
- w_out: float32 [2048, 4096], P(('fsdp', 'ctx'), 'tp'), may hold values from -0.09375 to 0.09375
- conv_x: float32 [4, 4096], P(None, 'tp'), may hold values from -3 to 3
- conv_x_bias: float32 [4096], P('tp'), may hold values from -3 to 3
- conv_bc: float32 [4, 256], replicated, may hold values from -3 to 3
- conv_bc_bias: float32 [256], replicated, may hold values from -3 to 3
- dt_bias: float32 [64], P('tp'), may hold values from -8 to -3
- a_log: float32 [64], P('tp'), may hold values from 0 to 2.5
- d_skip: float32 [64], P('tp'), may hold values from 0.5 to 1.5
- gate_gain: float32 [4096], P('tp'), may hold values from 0.5 to 1.5
Outputs:
- result: float32 [2048, 2048], P(('fsdp', 'ctx'), 'tp')
- grad_input: float32 [2048, 2048], P(('fsdp', 'ctx'), 'tp')
- grad_w_z: float32 [2048, 4096], P(('fsdp', 'ctx'), 'tp')
- grad_w_x: float32 [2048, 4096], P(('fsdp', 'ctx'), 'tp')
- grad_w_dt: float32 [2048, 64], P(('fsdp', 'ctx'), 'tp')
- grad_w_bc: float32 [2048, 256], P(('fsdp', 'ctx'))
- grad_w_out: float32 [2048, 4096], P(('fsdp', 'ctx'), 'tp')
- grad_conv_x: float32 [4, 4096], P(None, 'tp')
- grad_conv_x_bias: float32 [4096], P('tp')
- grad_conv_bc: float32 [4, 256], replicated
- grad_conv_bc_bias: float32 [256], replicated
- grad_dt_bias: float32 [64], P('tp')
- grad_a_log: float32 [64], P('tp')
- grad_d_skip: float32 [64], P('tp')
- grad_gate_gain: float32 [4096], P('tp')
- grad_gain_in: float32 [2048], P('tp')
Inputs may be any that keep to these rules, and one draw needn't show every extreme that they name: `seq_lengths`: the lengths of each row sum to 512; a length of zero is an empty slot; in every row one sequence covers positions 255 and 256. The slots are a permutation. The 256 tokens of arrival positions i * 256 to (i + 1) * 256 - 1 go to all 8 half rows (slot // 256), exactly 32 to each, so every half row receives exactly 32 tokens from each such block.
All inputs are finite; a program needn't handle non-finite values.
Results may differ from a plain program's by a relative error of at most 0.0003.
Values sent between devices are 32-bit elements; how exact they have to be, the bound alone decides.
A program may use at most 192 MiB of HBM per device.

v0:
```python
import jax
import jax.numpy as jnp
from jax import lax
from jax.sharding import PartitionSpec as P

N = 128
SPAN = 256
INNER = 4096


HIGH = lax.Precision.HIGHEST
EPSILON = 1e-05


def passed_along(block, axis, distance):
    devices = range(lax.axis_size(axis))
    route = [(i - distance, i) for i in devices if i - distance in devices]
    return lax.ppermute(block, axis, route)


def matmul(left, right):
    return jnp.dot(left, right, precision=HIGH)


def matmul_nt(left, right):
    return lax.dot_general(left, right, (((1,), (1,)), ((), ())), precision=HIGH)


def matmul_tn(left, right):
    return lax.dot_general(left, right, (((0,), (0,)), ((), ())), precision=HIGH)


def silu_f(value):
    return value * jax.nn.sigmoid(value)


def segment_of(positions, lengths):
    bounds = jnp.cumsum(lengths)
    hits = (bounds[None, :] <= positions[:, None]).astype(jnp.int32)
    return jnp.sum(hits, axis=1)


def norm_in(tokens, gain):
    scale = lax.rsqrt(jnp.mean(tokens * tokens, axis=1, keepdims=True) + EPSILON)
    return tokens * scale * gain[None, :]


def conv_act(pre, tail, taps, bias, raw_dt, dt_bias, a_log, segs, tail_segs, n_inner, n_state):
    extended = jnp.concatenate([tail, pre], axis=0)
    ext_segs = jnp.concatenate([tail_segs, segs])
    length = pre.shape[0]
    summed = jnp.zeros_like(pre) + bias[None, :]
    for offset_k in range(taps.shape[0]):
        moved = lax.slice_in_dim(extended, offset_k, offset_k + length, axis=0)
        same_doc = (lax.slice_in_dim(ext_segs, offset_k, offset_k + length, axis=0) == segs).astype(
            jnp.float32
        )
        summed = summed + taps[offset_k][None, :] * moved * same_doc[:, None]
    activated = silu_f(summed)
    xs = activated[:, :n_inner]
    bm = activated[:, n_inner : n_inner + n_state]
    cm = activated[:, n_inner + n_state :]
    step_size = jax.nn.softplus(raw_dt + dt_bias[None, :])
    decay_rate = -jnp.exp(a_log)
    return (xs, bm, cm, step_size, decay_rate)


def block_ssd(xs, step_size, decay_rate, bm, cm, d_skip, segs, seg_before, block_len):
    length, heads = step_size.shape
    head_width = xs.shape[1] // heads
    count = length // block_len
    x_blocks = xs.reshape(count, block_len, heads, head_width)
    log_blocks = (step_size * decay_rate[None, :]).reshape(count, block_len, heads)
    step_blocks = step_size.reshape(count, block_len, heads)
    b_blocks = bm.reshape(count, block_len, bm.shape[1])
    c_blocks = cm.reshape(count, block_len, cm.shape[1])
    seg_blocks = segs.reshape(count, block_len)
    seg_prev = jnp.concatenate([jnp.reshape(seg_before, (1,)), seg_blocks[:-1, -1]])
    rows_i = lax.broadcasted_iota(jnp.int32, (block_len, block_len), 0)
    cols_j = lax.broadcasted_iota(jnp.int32, (block_len, block_len), 1)

    def one_block(state, item):
        x_block, log_block, step_block, b_block, c_block, seg_block, seg_last_prev = item
        cumulative = jnp.cumsum(log_block, axis=0).T
        causal_same = (seg_block[:, None] == seg_block[None, :]) & (rows_i >= cols_j)
        gaps = cumulative[:, :, None] - cumulative[:, None, :]
        decays = jnp.where(causal_same[None], jnp.exp(jnp.where(causal_same[None], gaps, 0.0)), 0.0)
        scores = matmul_nt(c_block, b_block)
        weights = decays * scores[None] * step_block.T[:, None, :]
        mixed_out = jnp.einsum("hij,jhp->ihp", weights, x_block, precision=HIGH)
        keep_in = (seg_block == seg_last_prev).astype(jnp.float32)
        reading = jnp.exp(cumulative).T * keep_in[:, None]
        mixed_out = mixed_out + reading[:, :, None] * jnp.einsum(
            "in,hpn->ihp", c_block, state, precision=HIGH
        )
        last_seg = seg_block[-1]
        tail_w = (
            jnp.exp(cumulative[:, -1:] - cumulative).T
            * (seg_block == last_seg).astype(jnp.float32)[:, None]
            * step_block
        )
        carried = (jnp.exp(cumulative[:, -1]) * (last_seg == seg_last_prev).astype(jnp.float32))[
            :, None, None
        ] * state
        carried = carried + jnp.einsum("jh,jhp,jn->hpn", tail_w, x_block, b_block, precision=HIGH)
        mixed_out = mixed_out + d_skip[None, :, None] * x_block
        return (carried, mixed_out.reshape(block_len, heads * head_width))

    start_state = jnp.zeros((heads, head_width, bm.shape[1]), jnp.float32)
    end_state, outs = lax.scan(
        jax.checkpoint(one_block),
        start_state,
        (x_blocks, log_blocks, step_blocks, b_blocks, c_blocks, seg_blocks, seg_prev),
    )
    return (outs.reshape(length, heads * head_width), end_state)


def state_read(state, cm, step_size, decay_rate, segs, seg_before):
    cumulative = jnp.cumsum(step_size * decay_rate[None, :], axis=0)
    keep_in = (segs == seg_before).astype(jnp.float32)
    reading = jnp.exp(cumulative) * keep_in[:, None]
    read_out = reading[:, :, None] * jnp.einsum("in,hpn->ihp", cm, state, precision=HIGH)
    return read_out.reshape(cm.shape[0], -1)


def shards(
    inputs,
    cotangent,
    seq_lengths,
    slots,
    gain_in,
    w_z,
    w_x,
    w_dt,
    w_bc,
    w_out,
    conv_x,
    conv_x_bias,
    conv_bc,
    conv_bc_bias,
    dt_bias,
    a_log,
    d_skip,
    gate_gain,
):
    tok_count = inputs.shape[0]
    model_width = inputs.shape[1]
    groups = lax.axis_size(("fsdp", "ctx"))
    per_pair = tok_count // groups
    tp_count = lax.axis_size("tp")
    tp_index = lax.axis_index("tp")
    slice_width = model_width // tp_count
    targets = slots // tok_count
    onehot = (targets[:, None] == jnp.arange(groups, dtype=jnp.int32)[None, :]).astype(jnp.int32)
    ranks = jnp.sum((jnp.cumsum(onehot, axis=0) - onehot) * onehot, axis=1)
    send_at = targets * per_pair + ranks
    places = slots - targets * tok_count
    x_send = jnp.zeros((groups * per_pair, model_width), jnp.float32).at[send_at].set(inputs)
    c_send = jnp.zeros((groups * per_pair, model_width), jnp.float32).at[send_at].set(cotangent)
    p_send = jnp.full((groups * per_pair,), tok_count, jnp.int32).at[send_at].set(places)
    x_recv, c_recv, p_recv = (
        lax.all_to_all(
            x_send.reshape(groups, per_pair, model_width),
            ("fsdp", "ctx"),
            split_axis=0,
            concat_axis=0,
            tiled=True,
        ),
        lax.all_to_all(
            c_send.reshape(groups, per_pair, model_width),
            ("fsdp", "ctx"),
            split_axis=0,
            concat_axis=0,
            tiled=True,
        ),
        lax.all_to_all(
            p_send.reshape(groups, per_pair),
            ("fsdp", "ctx"),
            split_axis=0,
            concat_axis=0,
            tiled=True,
        ),
    )
    p_flat = p_recv.reshape(-1)
    tokens = (
        jnp.zeros((tok_count, model_width), jnp.float32)
        .at[p_flat]
        .set(x_recv.reshape(-1, model_width), mode="drop")
    )
    upstream = (
        jnp.zeros((tok_count, model_width), jnp.float32)
        .at[p_flat]
        .set(c_recv.reshape(-1, model_width), mode="drop")
    )
    gate_w, chan_w, step_w, state_w, proj_w = (
        lax.all_gather(w_z, ("fsdp", "ctx"), axis=0, tiled=True),
        lax.all_gather(w_x, ("fsdp", "ctx"), axis=0, tiled=True),
        lax.all_gather(w_dt, ("fsdp", "ctx"), axis=0, tiled=True),
        lax.all_gather(w_bc, ("fsdp", "ctx"), axis=0, tiled=True),
        lax.all_gather(w_out, ("fsdp", "ctx"), axis=0, tiled=True),
    )
    inner_local = gate_w.shape[1]
    lengths = seq_lengths[0]
    offset = lax.axis_index("ctx") * tok_count
    width = conv_x.shape[0]
    segs = segment_of(offset + jnp.arange(tok_count, dtype=jnp.int32), lengths)
    tail_segs = segment_of(offset - width + 1 + jnp.arange(width - 1, dtype=jnp.int32), lengths)
    seg_before = segment_of(jnp.reshape(offset - 1, (1,)), lengths)[0]
    normed, norm_back = jax.vjp(norm_in, tokens, gain_in)
    gate_pre = matmul(normed, gate_w)
    pre = jnp.concatenate([matmul(normed, chan_w), matmul(normed, state_w)], axis=1)
    raw_dt = matmul(normed, step_w)
    tail = passed_along(pre[tok_count - width + 1 :], "ctx", 1)
    taps = jnp.concatenate([conv_x, conv_bc], axis=1)
    bias = jnp.concatenate([conv_x_bias, conv_bc_bias])

    def act_fn(pre, tail, taps, bias, raw_dt, dt_bias, a_log):
        return conv_act(
            pre, tail, taps, bias, raw_dt, dt_bias, a_log, segs, tail_segs, inner_local, N
        )

    (xs, bm, cm, step_size, decay_rate), act_back = jax.vjp(
        act_fn, pre, tail, taps, bias, raw_dt, dt_bias, a_log
    )

    def ssd_fn(xs, step_size, decay_rate, bm, cm, d_skip):
        return block_ssd(xs, step_size, decay_rate, bm, cm, d_skip, segs, seg_before, SPAN)

    (y_own, end_state), ssd_back = jax.vjp(ssd_fn, xs, step_size, decay_rate, bm, cm, d_skip)
    state_in = passed_along(end_state, "ctx", 1)

    def read_fn(state, cm, step_size, decay_rate):
        return state_read(state, cm, step_size, decay_rate, segs, seg_before)

    y_read, read_back = jax.vjp(read_fn, state_in, cm, step_size, decay_rate)
    mixed = y_own + y_read
    gate_act = silu_f(gate_pre)
    gated = mixed * gate_act
    squares = jnp.sum(gated * gated, axis=1)
    shaped = gated * gate_gain[None, :]
    gscale = lax.rsqrt(lax.psum(squares, "tp") / INNER + EPSILON)
    shaped = shaped * gscale[:, None]
    partial_out = matmul_nt(shaped, proj_w)
    reduced = (lax.psum_scatter(partial_out, "tp", scatter_dimension=1, tiled=True),)
    branch_out = reduced[0]
    normal_y = gated * gscale[:, None] * gate_gain[None, :]
    own_cols = lax.dynamic_slice_in_dim(tokens, tp_index * slice_width, slice_width, 1)
    result_rows = own_cols + branch_out
    g_out = matmul_tn(upstream, normal_y)
    d_normal = matmul(upstream, proj_w)
    g_gate_gain = jnp.sum(d_normal * gated * gscale[:, None], axis=0)
    inner_part = jnp.sum(d_normal * gate_gain[None, :] * gated, axis=1)
    inner_total = lax.psum(inner_part, "tp")
    d_gated = (
        gscale[:, None] * gate_gain[None, :] * d_normal
        - gated * (gscale * gscale * gscale * inner_total / INNER)[:, None]
    )
    d_mixed = d_gated * gate_act
    sigmoid_z = jax.nn.sigmoid(gate_pre)
    d_gate_pre = d_gated * mixed * sigmoid_z * (1.0 + gate_pre * (1.0 - sigmoid_z))
    d_state_in, d_cm_read, d_step_read, d_rate_read = read_back(d_mixed)
    d_state_end = passed_along(d_state_in, "ctx", -1)
    d_xs, d_step_ssd, d_rate_ssd, d_bm_part, d_cm_ssd, g_skip = ssd_back((d_mixed, d_state_end))
    d_bm, d_cm = lax.psum((d_bm_part, d_cm_ssd + d_cm_read), "tp")
    d_pre, d_tail, g_taps, g_bias, d_raw_dt, g_dt_bias, g_a_log = act_back(
        (d_xs, d_bm, d_cm, d_step_ssd + d_step_read, d_rate_ssd + d_rate_read)
    )
    d_tail_in = passed_along(d_tail, "ctx", -1)
    d_pre = d_pre.at[tok_count - width + 1 :].add(d_tail_in)
    d_pre_x = d_pre[:, :inner_local]
    d_pre_bc = d_pre[:, inner_local:]
    lead_mask = (tp_index == 0).astype(jnp.float32)
    d_normed = (
        matmul_nt(d_gate_pre, gate_w)
        + matmul_nt(d_pre_x, chan_w)
        + matmul_nt(d_raw_dt, step_w)
        + matmul_nt(d_pre_bc * lead_mask, state_w)
    )
    g_gate_w = matmul_tn(normed, d_gate_pre)
    g_chan_w = matmul_tn(normed, d_pre_x)
    g_step_w = matmul_tn(normed, d_raw_dt)
    g_state_w = matmul_tn(normed, d_pre_bc)
    d_tokens_part, d_gain_part = norm_back(d_normed)
    d_tokens_own, d_gain_own = (
        lax.psum_scatter(d_tokens_part, "tp", scatter_dimension=1, tiled=True),
        lax.psum_scatter(d_gain_part, "tp", scatter_dimension=0, tiled=True),
    )
    up_cols = lax.dynamic_slice_in_dim(upstream, tp_index * slice_width, slice_width, 1)
    dx_rows = up_cols + d_tokens_own
    pad_row = jnp.zeros((1, slice_width), jnp.float32)
    out_send = jnp.concatenate([result_rows, pad_row], axis=0)[p_flat]
    dx_send = jnp.concatenate([dx_rows, pad_row], axis=0)[p_flat]
    out_back, dx_back = (
        lax.all_to_all(
            out_send.reshape(groups, per_pair, slice_width),
            ("fsdp", "ctx"),
            split_axis=0,
            concat_axis=0,
            tiled=True,
        ),
        lax.all_to_all(
            dx_send.reshape(groups, per_pair, slice_width),
            ("fsdp", "ctx"),
            split_axis=0,
            concat_axis=0,
            tiled=True,
        ),
    )
    result = out_back.reshape(-1, slice_width)[send_at]
    grad_input = dx_back.reshape(-1, slice_width)[send_at]
    s_gate_w, s_chan_w, s_step_w, s_state_w, s_out_w = (
        lax.psum_scatter(g_gate_w, ("fsdp", "ctx"), scatter_dimension=0, tiled=True),
        lax.psum_scatter(g_chan_w, ("fsdp", "ctx"), scatter_dimension=0, tiled=True),
        lax.psum_scatter(g_step_w, ("fsdp", "ctx"), scatter_dimension=0, tiled=True),
        lax.psum_scatter(g_state_w, ("fsdp", "ctx"), scatter_dimension=0, tiled=True),
        lax.psum_scatter(g_out, ("fsdp", "ctx"), scatter_dimension=0, tiled=True),
    )
    small_grads = lax.psum(
        (
            g_taps[:, :inner_local],
            g_bias[:inner_local],
            g_taps[:, inner_local:],
            g_bias[inner_local:],
            g_dt_bias,
            g_a_log,
            g_skip,
            g_gate_gain,
            d_gain_own,
        ),
        ("fsdp", "ctx"),
    )
    return (
        result,
        grad_input,
        s_gate_w,
        s_chan_w,
        s_step_w,
        s_state_w,
        s_out_w,
        small_grads[0],
        small_grads[1],
        small_grads[2],
        small_grads[3],
        small_grads[4],
        small_grads[5],
        small_grads[6],
        small_grads[7],
        small_grads[8],
    )


def solution(mesh):
    return jax.shard_map(
        shards,
        mesh=mesh,
        in_specs=(
            P(("fsdp", "ctx"), None),
            P(("fsdp", "ctx"), None),
            P("fsdp", None),
            P(("fsdp", "ctx")),
            P(),
            P(("fsdp", "ctx"), "tp"),
            P(("fsdp", "ctx"), "tp"),
            P(("fsdp", "ctx"), "tp"),
            P(("fsdp", "ctx"), None),
            P(("fsdp", "ctx"), "tp"),
            P(None, "tp"),
            P("tp"),
            P(),
            P(),
            P("tp"),
            P("tp"),
            P("tp"),
            P("tp"),
        ),
        out_specs=(
            P(("fsdp", "ctx"), "tp"),
            P(("fsdp", "ctx"), "tp"),
            P(("fsdp", "ctx"), "tp"),
            P(("fsdp", "ctx"), "tp"),
            P(("fsdp", "ctx"), "tp"),
            P(("fsdp", "ctx"), None),
            P(("fsdp", "ctx"), "tp"),
            P(None, "tp"),
            P("tp"),
            P(),
            P(),
            P("tp"),
            P("tp"),
            P("tp"),
            P("tp"),
            P("tp"),
        ),
        check_vma=False,
    )
```

profile of v0, /device:TPU:0, one launch (start us, length us, event | category | flops | bytes accessed | tf_op | source)
XLA Modules:
  0.0 781.6 jit_solution(3916518149548491110)
XLA Ops:
  13.1 5.2 all-to-all-start
  18.4 4.4 scatter_custom_fusion.1
  22.9 4.2 all-to-all-start.1
  29.7 4.3 scatter_custom_fusion.3
  34.1 28.7 %all_gather.15 = f32[2048,16]{0,1:T(8,128)S(1)} all-gather(f32[256,16]{0,1:T(8,128)S(1)} %copy-done.60), channel_id=1, replica_groups=mesh['fsdp'=4,'ctx'=2,'tp'=4] {'fsdp','ctx'}, dimensions={0}, use_global_device_ids=true | all-gather | bytes 147456 | tf_op jit(solution)/shard_map/all_gather | solution.py:198
  70.2 4.4 all-to-all-start.3
  74.6 3.7 scatter_custom_fusion.2
  83.3 3.6 fusion.138
  86.9 37.7 %all-gather.5.cloned.1.call-done = f32[2048,1024]{1,0:T(8,128)} async-done(((f32[256,1024]{1,0:T(8,128)}), f32[2048,1024]{1,0:T(8,128)}) %all-gather.5.cloned.1.call-update) | async-done | bytes 8388624 | tf_op jit(solution)/shard_map/all_gather | solution.py:197
  124.6 9.9 %fusion.139 = f32[256,1024]{1,0:T(8,128)S(1)} fusion(f32[2048,1024]{1,0:T(8,128)} %all-gather.5.cloned.1.call-done, f32[256,2048]{1,0:T(8,128)S(1)} %scatter_custom_fusion.2, f32[2048]{0:T(1024)S(1)} %copy-done.23, f32[256]{0:T(256)S(1)} %fusion.120), kind=kOutput, calls=%fused_computation.274 | convolution fusion | flops 6443499520 | bytes 11543552 | tf_op jit(solution)/shard_map/dot_general | solution.py:22
  135.5 2.7 collective-permute-start
  138.8 4.3 scatter_custom_fusion.4
  153.9 12.7 %collective-permute-start.1 = (f32[16,64,128]{2,1,0:T(8,128)S(1)}, f32[16,64,128]{2,1,0:T(8,128)S(1)}, u32[]{:S(2)}, u32[]{:S(2)}) collective-permute-start(f32[16,64,128]{2,1,0:T(8,128)S(1)} %convolution_add_fusion.3), channel_id=1, source_target_pairs={{0,4},{1,5},{2,6},{3,7},{8,12},{9,13},{10,14},{11,15},{16,20},{17,... | collective-permute-start | bytes 1572872 | tf_op jit(solution)/shard_map/ppermute | solution.py:18
  169.7 5.3 fusion.26
  177.1 3.1 multiply_add_fusion.1
  182.7 11.1 %multiply_reduce_fusion.14 = (f32[256]{0:T(256)S(1)}, f32[256,1024]{1,0:T(8,128)}, f32[256,1024]{1,0:T(8,128)}) fusion(f32[256,1024]{1,0:T(8,128)} %copy.96, f32[2048,1024]{1,0:T(8,128)} %all-gather.9.cloned.1.call-done, f32[256,2048]{1,0:T(8,128)S(1)} %scatter_custom_fusion.2, f32[2048]{0:T(1024)S(1)} %copy-done.23, f32[256]{0:T(256)S(1)} %fusion.120), kind=kOutput, calls=%fused_computation.94 | convolution fusion | flops 6445334528 | bytes 13641728 | tf_op jit(solution)/shard_map/dot_general | solution.py:22
  193.9 11.9 %psum.91 = f32[256]{0:T(256)S(1)} all-reduce(f32[256]{0:T(256)S(1)} %get-tuple-element.260), channel_id=1, replica_groups=mesh['fsdp'=4,'ctx'=2,'tp'=4] {'tp'}, use_global_device_ids=true, to_apply=%region_14.15 | all-reduce | flops 256 | bytes 2048 | tf_op jit(solution)/shard_map/psum | solution.py:241
  205.8 31.6 %all-gather.11.cloned.1.call-done = f32[2048,1024]{1,0:T(8,128)} async-done(((f32[256,1024]{1,0:T(8,128)}), f32[2048,1024]{1,0:T(8,128)}) %all-gather.11.cloned.1.call-update) | async-done | bytes 8388624 | tf_op jit(solution)/shard_map/all_gather | solution.py:200
  237.4 12.1 %multiply_reduce_fusion.10 = (f32[1024]{0:T(1024)}, f32[256]{0:T(256)S(1)}, f32[256,1024]{1,0:T(8,128)}) fusion(f32[256,1024]{1,0:T(8,128)} %get-tuple-element.261, f32[256]{0:T(256)S(1)} %add_rsqrt_fusion, f32[1024]{0:T(1024)S(1)} %copy-done.33, f32[256,2048]{1,0:T(8,128)} %scatter_custom_fusion.4, f32[2048,1024]{1,0:T(8,128)} %all-gather.11.cloned.1.call-done), kind=kOutput, calls=%fused_computation.81 | convolution fusion | flops 6444022784 | bytes 12593152 | tf_op jit(solution)/shard_map/dot_general | solution.py:22
  249.5 11.7 %psum.92 = f32[256]{0:T(256)S(1)} all-reduce(f32[256]{0:T(256)S(1)} %get-tuple-element.235), channel_id=1, replica_groups=mesh['fsdp'=4,'ctx'=2,'tp'=4] {'tp'}, use_global_device_ids=true, to_apply=%region_19.20 | all-reduce | flops 256 | bytes 2048 | tf_op jit(solution)/shard_map/psum | solution.py:253
  261.1 4.1 fusion.72
  267.7 3.1 fusion.66
  274.4 3.2 reduce-window.72
  278.3 3.8 convolution_bitcast_fusion.1
  299.6 3.7 multiply_reduce_fusion.11
  303.5 7.6 fusion.13
  322.5 4.2 reduce-window.70
  333.0 3.9 fusion.43
  336.8 3.2 fusion.42
  340.1 11.0 %fusion.49 = f32[256,2048]{1,0:T(8,128)} fusion(f32[2048,1024]{1,0:T(8,128)} %all-gather.11.cloned.1.call-done, f32[256,1024]{1,0:T(8,128)} %get-tuple-element.261, f32[256]{0:T(256)S(1)} %copy-done.41, f32[1024]{0:T(1024)S(1)} %copy-done.33), kind=kOutput, calls=%fused_computation.92 | convolution fusion | flops 6442975232 | bytes 11539456 | tf_op jit(solution)/shard_map/dot_general | solution.py:26
  351.2 11.2 %fusion.145 = f32[256,2048]{1,0:T(8,128)} fusion(f32[256,1024]{1,0:T(8,128)} %get-tuple-element.267, f32[2048,1024]{1,0:T(8,128)} %all-gather.9.cloned.1.call-done), kind=kOutput, calls=%fused_computation.277 | convolution fusion | flops 6442450944 | bytes 11534336 | tf_op jit(solution)/shard_map/dot_general | solution.py:26
  362.5 4.8 fusion.34
  369.9 4.7 all-reduce.20.cloned.1.call-done
  374.6 3.5 multiply_reduce_fusion.7
  382.2 10.5 %convolution_add_fusion.2 = f32[256,2048]{1,0:T(8,128)S(1)} fusion(f32[256,2048]{1,0:T(8,128)} %fusion.145, f32[2048,1024]{1,0:T(8,128)} %all-gather.5.cloned.1.call-done, f32[256,1280]{1,0:T(8,128)S(1)} %scatter-add.4), kind=kOutput, calls=%fused_computation.27 | convolution fusion | flops 6442975232 | bytes 13631488 | tf_op jit(solution)/shard_map/dot_general | solution.py:26
  401.4 4.9 fusion.81
  407.6 10.5 %fusion.44 = f32[2048,1024]{1,0:T(8,128)} fusion(f32[256,2048]{1,0:T(8,128)} %scatter_custom_fusion.4, f32[256,1024]{1,0:T(8,128)S(1)} %copy-done, f32[256]{0:T(256)S(1)} %copy-done.41, f32[1024]{0:T(1024)S(1)} %copy-done.33), kind=kOutput, calls=%fused_computation.83 | convolution fusion | flops 6442975232 | bytes 11539456 | tf_op jit(solution)/shard_map/dot_general | solution.py:30
  419.3 9.1 %fusion.136 = f32[2048,1024]{1,0:T(8,128)} fusion(f32[256,1024]{1,0:T(8,128)S(1)} %copy-done.12, f32[256,2048]{1,0:T(8,128)S(1)} %scatter_custom_fusion.2, f32[2048]{0:T(1024)S(1)} %copy-done.23, f32[256]{0:T(256)S(1)} %fusion.120), kind=kOutput, calls=%fused_computation.271 | convolution fusion | flops 6443499520 | bytes 11543552 | tf_op jit(solution)/shard_map/dot_general | solution.py:30
  429.7 9.1 %fusion.62 = f32[2048,1024]{1,0:T(8,128)} fusion(f32[256,1280]{1,0:T(8,128)S(1)} %copy-done.10, f32[256,2048]{1,0:T(8,128)S(1)} %scatter_custom_fusion.2, f32[2048]{0:T(1024)S(1)} %copy-done.23, f32[256]{0:T(256)S(1)} %fusion.120), kind=kOutput, calls=%fused_computation.108 | convolution fusion | flops 6443499520 | bytes 11543552 | tf_op jit(solution)/shard_map/dot_general | solution.py:30
  442.5 3.7 all-to-all-start.2
  447.5 18.5 %reduce-scatter.10.cloned.1.call-done = f32[256,512]{1,0:T(8,128)} async-done(((f32[256,2048]{1,0:T(8,128)}), f32[256,512]{1,0:T(8,128)}) %reduce-scatter.10.cloned.1.call-update) | async-done | bytes 524304 | tf_op jit(solution)/shard_map/reduce_scatter | solution.py:285
  469.2 3.7 all-to-all-start.4
  473.1 10.2 %all-reduce.15 = f32[2048]{0:T(1024)S(1)} all-reduce(f32[2048]{0:T(1024)S(1)} %get-tuple-element.229), channel_id=9, replica_groups=mesh['fsdp'=4,'ctx'=2,'tp'=4] {'tp'}, use_global_device_ids=true, to_apply=%region_62.63.clone | all-reduce | flops 2048 | bytes 16384
  483.3 23.8 %all-reduce.16 = (f32[4,1024]{1,0:T(4,128)}, f32[1024]{0:T(1024)}, f32[4,256]{1,0:T(4,128)}, f32[256]{0:T(256)}, f32[16]{0:T(128)}, /*index=5*/f32[16]{0:T(128)}, f32[16]{0:T(128)}, f32[1024]{0:T(1024)}, f32[512]{0:T(512)}) all-reduce(f32[4,1024]{1,0:T(4,128)S(1)} %slice.213, ...), channel_id=1, replica_groups=mesh['fsdp'=4,'ctx'=2,'tp'=4] {'fsdp','ctx'}, use_global_device_ids=true, to_apply=%region_47.48 | all-reduce | flops 7984 | bytes 63872 | tf_op jit(solution)/shard_map/psum | solution.py:318
  510.7 37.0 %reduce-scatter.18.cloned.1.call-done = f32[256,256]{1,0:T(8,128)} async-done(((f32[2048,256]{1,0:T(8,128)}), f32[256,256]{1,0:T(8,128)}) %reduce-scatter.18.cloned.1.call-update) | async-done | bytes 262160 | tf_op jit(solution)/shard_map/reduce_scatter | solution.py:315
  547.6 75.6 %reduce-scatter.20.cloned.1.call-done = f32[256,1024]{1,0:T(8,128)} async-done(((f32[2048,1024]{1,0:T(8,128)}), f32[256,1024]{1,0:T(8,128)}) %reduce-scatter.20.cloned.1.call-update) | async-done | bytes 1048592 | tf_op jit(solution)/shard_map/reduce_scatter | solution.py:316
  623.3 75.3 %reduce-scatter.12.cloned.1.call-done = f32[256,1024]{1,0:T(8,128)} async-done(((f32[2048,1024]{1,0:T(8,128)}), f32[256,1024]{1,0:T(8,128)}) %reduce-scatter.12.cloned.1.call-update) | async-done | bytes 1048592 | tf_op jit(solution)/shard_map/reduce_scatter | solution.py:312
  698.6 75.6 %reduce-scatter.14.cloned.1.call-done = f32[256,1024]{1,0:T(8,128)} async-done(((f32[2048,1024]{1,0:T(8,128)}), f32[256,1024]{1,0:T(8,128)}) %reduce-scatter.14.cloned.1.call-update) | async-done | bytes 1048592 | tf_op jit(solution)/shard_map/reduce_scatter | solution.py:313
  (353 shorter events, 110.5 us)
Async XLA Ops:
  7.2 76.1 %all-gather.7.cloned.1.call-start = ((), (), s32[]{:S(2)}) async-start(), calls=%async_computation.13 | async-start | bytes 2359296 | tf_op jit(solution)/shard_map/all_gather | solution.py:199
  7.9 116.7 %all-gather.5.cloned.1.call-start = ((), (), s32[]{:S(2)}) async-start(), calls=%async_computation.12 | async-start | bytes 9437184 | tf_op jit(solution)/shard_map/all_gather | solution.py:197
  8.7 174.0 %all-gather.9.cloned.1.call-start = ((), (), s32[]{:S(2)}) async-start(), calls=%async_computation.14 | async-start | bytes 9437184 | tf_op jit(solution)/shard_map/all_gather | solution.py:196
  9.4 228.0 %all-gather.11.cloned.1.call-start = ((), (), s32[]{:S(2)}) async-start(), calls=%async_computation.15 | async-start | bytes 9437184 | tf_op jit(solution)/shard_map/all_gather | solution.py:200
  11.0 18.7 %copy-start.75 = (s32[256]{0:T(256)}, s32[256]{0:T(256)S(1)}, u32[]{:S(2)}) copy-start(s32[256]{0:T(256)S(1)} %compare_select_fusion.6) | copy-start | bytes 3076
  13.1 9.8 %all-to-all-start = ((s32[8,1,32]{2,1,0:T(1,128)}), s32[8,1,32]{2,1,0:T(1,128)S(1)}, u32[]{:S(2)}, u32[]{:S(2)}) async-start(s32[8,1,32]{2,1,0:T(1,128)} %all_to_all.18), calls=%async_computation | async-start | bytes 8192 | tf_op jit(solution)/shard_map/all_to_all | solution.py:176
  22.9 46.0 %all-to-all-start.1 = ((f32[8,32,2048]{2,1,0:T(8,128)}), f32[8,32,2048]{2,1,0:T(8,128)S(1)}, u32[]{:S(2)}, u32[]{:S(2)}) async-start(f32[8,32,2048]{2,1,0:T(8,128)} %bitcast.4), calls=%async_computation.1 | async-start | bytes 4194304 | tf_op jit(solution)/shard_map/all_to_all | solution.py:162
  27.1 36.0 %copy-start.62 = (f32[4,1024]{1,0:T(4,128)S(1)}, f32[4,1024]{1,0:T(4,128)}, u32[]{:S(2)}) copy-start(f32[4,1024]{1,0:T(4,128)} %param.30) | copy-start | bytes 49156
  27.1 36.0 %copy-start.78 = (f32[4,256]{1,0:T(4,128)S(1)}, f32[4,256]{1,0:T(4,128)}, u32[]{:S(2)}) copy-start(f32[4,256]{1,0:T(4,128)} %param.32) | copy-start | bytes 12292
  27.1 36.0 %copy-start.79 = (f32[1024]{0:T(1024)S(1)}, f32[1024]{0:T(1024)}, u32[]{:S(2)}) copy-start(f32[1024]{0:T(1024)} %param.31) | copy-start | bytes 12292
  27.1 36.0 %copy-start.85 = (f32[256]{0:T(256)S(1)}, f32[256]{0:T(256)}, u32[]{:S(2)}) copy-start(f32[256]{0:T(256)} %param.33) | copy-start | bytes 3076
  27.1 37.2 %copy-start.90 = (f32[16]{0:T(128)S(1)}, f32[16]{0:T(128)}, u32[]{:S(2)}) copy-start(f32[16]{0:T(128)} %param.35) | copy-start | bytes 196
  27.2 41.7 %copy-start.45 = (s32[256]{0:T(256)}, s32[256]{0:T(256)S(1)}, u32[]{:S(2)}) copy-start(s32[256]{0:T(256)S(1)} %convert_reduce_fusion) | copy-start | bytes 3076
  62.8 15.8 %copy-start.24 = (f32[2048,16]{0,1:T(8,128)}, f32[2048,16]{0,1:T(8,128)S(1)}, u32[]{:S(2)}) copy-start(f32[2048,16]{0,1:T(8,128)S(1)} %all_gather.15) | copy-start | bytes 393220
  64.3 80.3 %copy-start.34 = (f32[1280]{0:T(1024)}, f32[1280]{0:T(1024)S(1)}, u32[]{:S(2)}) copy-start(f32[1280]{0:T(1024)S(1)} %get-tuple-element.241) | copy-start | bytes 15364
  64.3 80.3 %copy-start.36 = (f32[1280]{0:T(1024)}, f32[1280]{0:T(1024)S(1)}, u32[]{:S(2)}) copy-start(f32[1280]{0:T(1024)S(1)} %get-tuple-element.242) | copy-start | bytes 15364
  64.3 18.2 %copy-start.74 = (f32[16]{0:T(128)}, f32[16]{0:T(128)S(1)}, u32[]{:S(2)}) copy-start(f32[16]{0:T(128)S(1)} %exponential_negate_fusion) | copy-start | bytes 196
  66.3 16.2 %copy-start.71 = (f32[256]{0:T(256)}, f32[256]{0:T(256)S(1)}, u32[]{:S(2)}) copy-start(f32[256]{0:T(256)S(1)} %get-tuple-element.293) | copy-start | bytes 3076
  70.2 68.6 %all-to-all-start.3 = ((f32[8,32,2048]{2,1,0:T(8,128)}), f32[8,32,2048]{2,1,0:T(8,128)}, u32[]{:S(2)}, u32[]{:S(2)}) async-start(f32[8,32,2048]{2,1,0:T(8,128)} %bitcast.21), calls=%async_computation.4 | async-start | bytes 4194304 | tf_op jit(solution)/shard_map/all_to_all | solution.py:169
  74.6 300.0 %all-reduce.20.cloned.1.call-start = ((), (), s32[]{:S(2)}) async-start(), calls=%async_computation.23 | async-start | bytes 524288 | tf_op jit(solution)/shard_map/psum | solution.py:264
  86.9 47.6 %copy-start.17 = (f32[256,256]{1,0:T(8,128)}, f32[256,256]{1,0:T(8,128)S(1)}, u32[]{:S(2)}) copy-start(f32[256,256]{1,0:T(8,128)S(1)} %fusion.138) | copy-start | bytes 786436
  135.5 7.6 collective-permute-start
  151.6 18.1 %copy-start.1 = (f32[256,1024]{0,1:T(8,128)S(1)}, f32[256,1024]{0,1:T(8,128)}, u32[]{:S(2)}) copy-start(f32[256,1024]{0,1:T(8,128)} %copy.95) | copy-start | bytes 3145732
  151.6 18.1 %copy-start.49 = (pred[256,256]{1,0:T(8,128)(4,1)S(1)}, pred[256,256]{1,0:T(8,128)(4,1)}, u32[]{:S(2)}) copy-start(pred[256,256]{1,0:T(8,128)(4,1)} %fusion.80) | copy-start | bytes 196612
  151.6 18.1 %copy-start.53 = (f32[16,256]{1,0:T(8,128)S(1)}, f32[16,256]{1,0:T(8,128)}, u32[]{:S(2)}) copy-start(f32[16,256]{1,0:T(8,128)} %copy-done.52) | copy-start | bytes 49156
  151.6 18.1 %copy-start.61 = (f32[16,256]{1,0:T(8,128)S(1)}, f32[16,256]{1,0:T(8,128)}, u32[]{:S(2)}) copy-start(f32[16,256]{1,0:T(8,128)} %get-tuple-element.284) | copy-start | bytes 49156
  153.9 21.1 %collective-permute-start.1 = (f32[16,64,128]{2,1,0:T(8,128)S(1)}, f32[16,64,128]{2,1,0:T(8,128)S(1)}, u32[]{:S(2)}, u32[]{:S(2)}) collective-permute-start(f32[16,64,128]{2,1,0:T(8,128)S(1)} %convolution_add_fusion.3), channel_id=1, source_target_pairs={{0,4},{1,5},{2,6},{3,7},{8,12},{9,13},{10,14},{11,15},{16,20},{17,... | collective-permute-start | bytes 1572872 | tf_op jit(solution)/shard_map/ppermute | solution.py:18
  182.7 54.7 %copy-start.33 = (f32[1024]{0:T(1024)S(1)}, f32[1024]{0:T(1024)}, u32[]{:S(2)}) copy-start(f32[1024]{0:T(1024)} %param.37) | copy-start | bytes 12292
  205.8 55.3 %copy-start.40 = (f32[256]{0:T(256)}, f32[256]{0:T(256)S(1)}, u32[]{:S(2)}) copy-start(f32[256]{0:T(256)S(1)} %add_rsqrt_fusion) | copy-start | bytes 3076
  270.8 11.3 %collective-permute-start.2 = (f32[16,64,128]{2,1,0:T(8,128)}, f32[16,64,128]{2,1,0:T(8,128)}, u32[]{:S(2)}, u32[]{:S(2)}) collective-permute-start(f32[16,64,128]{2,1,0:T(8,128)} %fusion.66), channel_id=1, source_target_pairs={{4,0},{5,1},{6,2},{7,3},{12,8},{13,9},{14,10},{15,11},{20,16},{21,... | collective-permute-start | bytes 1572872 | tf_op jit(solution)/shard_map/ppermute | solution.py:18
  340.0 99.5 %reduce-scatter.8.cloned.1.call-start = ((), (), s32[]{:S(2)}) async-start(), calls=%async_computation.16 | async-start | bytes 2621440 | tf_op jit(solution)/shard_map/reduce_scatter | solution.py:244
  351.1 114.9 %reduce-scatter.10.cloned.1.call-start = ((), (), s32[]{:S(2)}) async-start(), calls=%async_computation.17 | async-start | bytes 2621440 | tf_op jit(solution)/shard_map/reduce_scatter | solution.py:285
  351.2 11.3 %copy-start.8 = (f32[256,1024]{0,1:T(8,128)S(1)}, f32[256,1024]{0,1:T(8,128)}, u32[]{:S(2)}) copy-start(f32[256,1024]{0,1:T(8,128)} %copy.101) | copy-start | bytes 3145732
  351.2 11.3 %copy-start.28 = (f32[256,16,64]{0,2,1:T(8,128)S(1)}, f32[256,16,64]{0,2,1:T(8,128)}, u32[]{:S(2)}) copy-start(f32[256,16,64]{0,2,1:T(8,128)} %get-tuple-element.300) | copy-start | bytes 3145732
  351.2 11.3 %copy-start.32 = (f32[256,256]{1,0:T(8,128)S(1)}, f32[256,256]{1,0:T(8,128)}, u32[]{:S(2)}) copy-start(f32[256,256]{1,0:T(8,128)} %copy-done.31) | copy-start | bytes 786436
  351.2 11.3 %copy-start.43 = (f32[256,16]{0,1:T(8,128)S(1)}, f32[256,16]{0,1:T(8,128)}, u32[]{:S(2)}) copy-start(f32[256,16]{0,1:T(8,128)} %copy-done.42) | copy-start | bytes 49156
  378.6 3.1 collective-permute-start.3
  382.1 19.3 %copy-start.9 = (f32[256,1280]{1,0:T(8,128)}, f32[256,1280]{1,0:T(8,128)S(1)}, u32[]{:S(2)}) copy-start(f32[256,1280]{1,0:T(8,128)S(1)} %scatter-add.4) | copy-start | bytes 3932164
  399.0 111.7 %reduce-scatter.16.cloned.1.call-start = ((), (), s32[]{:S(2)}) async-start(), calls=%async_computation.20 | async-start | bytes 147456 | tf_op jit(solution)/shard_map/reduce_scatter | solution.py:314
  401.1 146.5 %reduce-scatter.18.cloned.1.call-start = ((), (), s32[]{:S(2)}) async-start(), calls=%async_computation.21 | async-start | bytes 2359296 | tf_op jit(solution)/shard_map/reduce_scatter | solution.py:315
  406.4 216.9 %reduce-scatter.20.cloned.1.call-start = ((), (), s32[]{:S(2)}) async-start(), calls=%async_computation.22 | async-start | bytes 9437184 | tf_op jit(solution)/shard_map/reduce_scatter | solution.py:316
  418.1 280.5 %reduce-scatter.12.cloned.1.call-start = ((), (), s32[]{:S(2)}) async-start(), calls=%async_computation.18 | async-start | bytes 9437184 | tf_op jit(solution)/shard_map/reduce_scatter | solution.py:312
  428.4 345.8 %reduce-scatter.14.cloned.1.call-start = ((), (), s32[]{:S(2)}) async-start(), calls=%async_computation.19 | async-start | bytes 9437184 | tf_op jit(solution)/shard_map/reduce_scatter | solution.py:313
  442.5 26.7 %all-to-all-start.2 = ((f32[8,32,512]{2,1,0:T(8,128)}), f32[8,32,512]{2,1,0:T(8,128)S(1)}, u32[]{:S(2)}, u32[]{:S(2)}) async-start(f32[8,32,512]{2,1,0:T(8,128)} %bitcast.19), calls=%async_computation.3 | async-start | bytes 1048576 | tf_op jit(solution)/shard_map/all_to_all | solution.py:294
  467.4 16.0 %copy-start.59 = (f32[1024]{0:T(1024)S(1)}, f32[1024]{0:T(1024)}, u32[]{:S(2)}) copy-start(f32[1024]{0:T(1024)} %get-tuple-element.234) | copy-start | bytes 12292
  467.4 16.0 %copy-start.80 = (f32[16]{0:T(128)S(1)}, f32[16]{0:T(128)}, u32[]{:S(2)}) copy-start(f32[16]{0:T(128)} %get-tuple-element.238) | copy-start | bytes 196
  467.4 16.0 %copy-start.81 = (f32[16]{0:T(128)S(1)}, f32[16]{0:T(128)}, u32[]{:S(2)}) copy-start(f32[16]{0:T(128)} %get-tuple-element.274) | copy-start | bytes 196
  469.2 39.7 %all-to-all-start.4 = ((f32[8,32,512]{2,1,0:T(8,128)}), f32[8,32,512]{2,1,0:T(8,128)S(1)}, u32[]{:S(2)}, u32[]{:S(2)}) async-start(f32[8,32,512]{2,1,0:T(8,128)} %bitcast.47), calls=%async_computation.6 | async-start | bytes 1048576 | tf_op jit(solution)/shard_map/all_to_all | solution.py:301
  (67 other events, 318.7 us)
Sparse Core Ops, SparseCore 0:
  9.9 41.9 all-gather.6
  53.8 70.7 all-gather.4
  126.5 54.6 all-gather.8
  183.0 54.3 all-gather.10
  340.2 34.3 all-reduce.19
  376.8 43.6 reduce-scatter.7
  422.8 43.1 reduce-scatter.9
  469.8 32.6 reduce-scatter.15
  506.4 41.1 reduce-scatter.17
  551.9 71.3 reduce-scatter.19
  627.3 71.2 reduce-scatter.11
  702.9 71.2 reduce-scatter.13
where the time goes:
time: 790 us; the launch traced here: 782 us
  waiting for transfers between devices  360 us (46%)
  matrix products  162 us (21%)
  blocking collectives  86.3 us (11%)
  local copies, waits for them, and re-layouts  64.1 us (8%)
  other arithmetic  49.8 us (6%)
  starting transfers between devices  40.4 us (5%)
  between operations  19.2 us (2%)
    reduce_scatter x1, waiting for transfers between devices, shards(): lax.psum_scatter(g_out, ('fsdp', 'ctx'), scatter_dimension=0, tiled=True)  75.6 us
    reduce_scatter x1, waiting for transfers between devices, shards(): lax.psum_scatter(g_chan_w, ('fsdp', 'ctx'), scatter_dimension=0, tiled=True)  75.6 us
    reduce_scatter x1, waiting for transfers between devices, shards(): lax.psum_scatter(g_gate_w, ('fsdp', 'ctx'), scatter_dimension=0, tiled=True)  75.3 us
    dot_general x9, matrix products, matmul_nt(): lax.dot_general(left, right, (((1,), (1,)), ((), ())), precision=HIGH)  42.3 us
    dot_general x5, matrix products, matmul(): return jnp.dot(left, right, precision=HIGH)  38.6 us
    all_gather x1, waiting for transfers between devices, shards(): lax.all_gather(w_x, ('fsdp', 'ctx'), axis=0, tiled=True)  37.7 us
    reduce_scatter x1, waiting for transfers between devices, shards(): lax.psum_scatter(g_state_w, ('fsdp', 'ctx'), scatter_dimension=0, tiled=T...  37 us
    dot_general x5, matrix products, matmul_tn(): lax.dot_general(left, right, (((0,), (0,)), ((), ())), precision=HIGH)  35.7 us
  transfers between devices with their start and end apart: 21, of which 9 were waited for; matrix products, arithmetic and copies ran while one was open for 24% of the time, Pallas kernels for 0%

commit v1 on v0

--- a/solution.py
+++ b/solution.py
@@ -1,15 +1,425 @@
+import functools
+import math
+
 import jax
 import jax.numpy as jnp
 from jax import lax
+from jax.experimental import pallas as pl
+from jax.experimental.pallas import tpu as pltpu
 from jax.sharding import PartitionSpec as P
 
 N = 128
 SPAN = 256
 INNER = 4096
-
-
-HIGH = lax.Precision.HIGHEST
 EPSILON = 1e-05
+F32 = jnp.float32
+BF16 = jnp.bfloat16
+MESH = pl.DeviceIdType.MESH
+NN = (((1,), (0,)), ((), ()))
+NT = (((1,), (1,)), ((), ()))
+TN = (((0,), (0,)), ((), ()))
+VMEM_LIMIT = 62 << 20
+
+
+def split2(value):
+    high = value.astype(BF16)
+    return high, (value - high.astype(F32)).astype(BF16)
+
+
+def split3(value):
+    high = value.astype(BF16)
+    rest = value - high.astype(F32)
+    middle = rest.astype(BF16)
+    return high, middle, (rest - middle.astype(F32)).astype(BF16)
+
+
+def dot1(left, right, dims):
+    return lax.dot_general(left, right, dims, preferred_element_type=F32)
+
+
+def dot_split(left, right, dims):
+    (lh, ll), (rh, rl) = left, right
+    return dot1(lh, rh, dims) + (dot1(lh, rl, dims) + dot1(ll, rh, dims))
+
+
+def dot3(left, right, dims):
+    return dot_split(split2(left), split2(right), dims)
+
+
+def pick(table, value, dims):
+    parts = split3(value)
+    return dot1(table, parts[0], dims) + dot1(table, parts[1], dims) + dot1(table, parts[2], dims)
+
+
+def iota(shape, dim):
+    return lax.broadcasted_iota(jnp.int32, shape, dim)
+
+
+class Place:
+    def __init__(self, fsdp, ctx, tp):
+        self.fsdp, self.n_ctx, self.tp = fsdp, ctx, tp
+        self.side = math.isqrt(fsdp)
+        assert self.side * self.side == fsdp and ctx == 2
+        self.f = lax.axis_index("fsdp")
+        self.c = lax.axis_index("ctx")
+        self.z = lax.axis_index("tp")
+        self.y, self.x = self.f // self.side, self.f % self.side
+
+    def chip(self, dy, dx):
+        side = self.side
+        return ((self.y + dy + side) % side) * side + (self.x + dx + side) % side
+
+    def block(self, dy, dx, core):
+        return self.chip(dy, dx) * 2 + core
+
+    def at(self, dy, dx):
+        return (self.chip(dy, dx), self.c, self.z)
+
+    def sibling(self):
+        return (self.f, 1 - self.c, self.z)
+
+    def plane(self):
+        out = []
+        for df in range(self.fsdp):
+            for dc in range(2):
+                if df or dc:
+                    to_f = (self.f + df) % self.fsdp
+                    from_f = (self.f - df + self.fsdp) % self.fsdp
+                    core = (self.c + dc) % 2
+                    out.append(((to_f, core, self.z), to_f * 2 + core, from_f * 2 + core))
+        return out
+
+    def column(self):
+        out = []
+        for dz in range(1, self.tp):
+            to_z = (self.z + dz) % self.tp
+            out.append(((self.f, self.c, to_z), to_z, (self.z - dz + self.tp) % self.tp))
+        return out
+
+
+class Links:
+    def __init__(self, send, recv, local):
+        self.send, self.recv, self.local = send, recv, local
+        self.used, self.used_local = 0, 0
+        self.open = []
+
+    def remote(self, src, dst, device):
+        k = self.used
+        self.used += 1
+        copy = pltpu.make_async_remote_copy(
+            src_ref=src,
+            dst_ref=dst,
+            send_sem=self.send.at[k],
+            recv_sem=self.recv.at[k],
+            device_id=device,
+            device_id_type=MESH,
+        )
+        copy.start()
+        self.open.append(copy)
+        return copy
+
+    def move(self, src, dst):
+        k = self.used_local
+        self.used_local += 1
+        copy = pltpu.make_async_copy(src, dst, self.local.at[k])
+        copy.start()
+        return copy
+
+    def finish(self):
+        for copy in self.open:
+            copy.wait_send()
+
+
+def greet(devices):
+    barrier = pltpu.get_barrier_semaphore()
+    for device in devices:
+        pl.semaphore_signal(barrier, inc=1, device_id=device, device_id_type=MESH)
+    pl.semaphore_wait(barrier, len(devices))
+
+
+class Gather:
+    def __init__(self, place, links, shard, whole):
+        self.place, self.links, self.shard, self.whole = place, links, shard, whole
+        self.rows = shard.shape[0]
+
+    def rows_of(self, block, start=0, count=None):
+        count = self.rows if count is None else count
+        return self.whole.at[pl.ds(pl.multiple_of(block * self.rows + start, 8), count)]
+
+    def start(self):
+        p, steps = self.place, range(1, self.place.side)
+        mine = self.rows_of(p.block(0, 0, p.c))
+        self.row = [self.links.remote(self.shard, mine, p.at(0, d)) for d in steps]
+        self.col = [self.links.remote(self.shard, mine, p.at(d, 0)) for d in steps]
+        self.pair = [self.links.remote(self.shard, mine, p.sibling())]
+        self.own = self.links.move(self.shard, mine)
+
+    def forward(self):
+        p, steps, half = self.place, range(1, self.place.side), self.rows // 2
+        self.half_a, self.half_b = [], []
+        for k, d in enumerate(steps):
+            self.row[k].wait_recv()
+            block = p.block(0, -d, p.c)
+            part = self.rows_of(block, 0, half)
+            self.half_a += [self.links.remote(part, part, p.at(e, 0)) for e in steps]
+            whole = self.rows_of(block)
+            self.pair.append(self.links.remote(whole, whole, p.sibling()))
+        for k, e in enumerate(steps):
+            self.col[k].wait_recv()
+            block = p.block(-e, 0, p.c)
+            part = self.rows_of(block, half, half)
+            self.half_b += [self.links.remote(part, part, p.at(0, d)) for d in steps]
+            whole = self.rows_of(block)
+            self.pair.append(self.links.remote(whole, whole, p.sibling()))
+
+    def share(self):
+        p, steps, half = self.place, range(1, self.place.side), self.rows // 2
+        k = 0
+        for d in steps:
+            for e in steps:
+                self.half_a[k].wait_recv()
+                part = self.rows_of(p.block(-e, -d, p.c), 0, half)
+                self.pair.append(self.links.remote(part, part, p.sibling()))
+                k += 1
+        k = 0
+        for e in steps:
+            for d in steps:
+                self.half_b[k].wait_recv()
+                part = self.rows_of(p.block(-e, -d, p.c), half, half)
+                self.pair.append(self.links.remote(part, part, p.sibling()))
+                k += 1
+
+    def finish(self):
+        self.own.wait()
+        for copy in self.pair:
+            copy.wait_recv()
+
+
+def gather_copies(side):
+    steps = side - 1
+    return 4 * steps + 1 + 4 * steps * steps
+
+
+def project(left_high, left_low, whole, out, tile):
+    slices, _, width = left_high.shape
+
+    @pl.loop(0, whole.shape[1] // tile)
+    def _(n):
+        cols = pl.ds(pl.multiple_of(n * tile, 128), tile)
+        total = jnp.zeros((left_high.shape[1], tile), F32)
+        for k in range(slices):
+            right = split2(whole[k * width : (k + 1) * width, cols])
+            total = total + dot_split((left_high[k], left_low[k]), right, NN)
+        out[:, cols] = total
+
+
+def forward_kernel(
+    sizes,
+    slots_in,
+    gain,
+    x_in,
+    c_in,
+    w_x,
+    w_s,
+    w_z,
+    w_out,
+    tokens_out,
+    upstream_out,
+    p_recv,
+    pre_x,
+    pre_s,
+    gate_pre,
+    d_normal,
+    wx_out,
+    ws_out,
+    wz_out,
+    wo_out,
+    wx,
+    ws,
+    wz,
+    wo,
+    x_own,
+    c_own,
+    x_sort,
+    c_sort,
+    p_sort,
+    x_recv,
+    c_recv,
+    tokens,
+    upstream,
+    n_high,
+    n_low,
+    send,
+    recv,
+    local,
+):
+    place = Place(*sizes)
+    links = Links(send, recv, local)
+    tok, groups = x_own.shape[0], 2 * place.fsdp
+    per_pair = tok // groups
+    slice_width = x_own.shape[1]
+    slice_cols = pl.ds(pl.multiple_of(place.z * slice_width, 128), slice_width)
+    load_x = links.move(x_in.at[:, slice_cols], x_own)
+    load_c = links.move(c_in.at[:, slice_cols], c_own)
+    plane, column = place.plane(), place.column()
+    greet([entry[0] for entry in plane] + [entry[0] for entry in column])
+
+    gathers = [Gather(place, links, shard, whole) for shard, whole in ((w_x, wx), (w_s, ws), (w_z, wz), (w_out, wo))]
+    g_x, g_s, g_z, g_o = gathers
+    g_x.start()
+    g_s.start()
+
+    slots = slots_in[...]
+    targets = slots >> (tok.bit_length() - 1)
+    member = (targets == iota((tok, 128), 1)).astype(F32)
+    earlier = (iota((tok, tok), 0) > iota((tok, tok), 1)).astype(BF16)
+    ranks = jnp.sum(dot1(earlier, member.astype(BF16), NN) * member, axis=1, keepdims=True)
+    send_at = (targets[:, :1] * per_pair).astype(F32) + ranks
+    leave = (send_at == iota((tok, tok), 1).astype(F32)).astype(BF16)
+    place_of = (slots - targets * tok).astype(F32).astype(BF16)
+    p_sort[...] = dot1(leave, place_of, TN)
+    load_x.wait()
+    x_sort[...] = pick(leave, x_own[...], TN)
+
+    def rows(group):
+        return pl.ds(pl.multiple_of(group * per_pair, 8), per_pair)
+
+    def route(source, target):
+        mine = rows(place.f * 2 + place.c)
+        copies = [links.remote(source.at[rows(to)], target.at[mine], device) for device, to, _ in plane]
+        return copies, links.move(source.at[mine], target.at[mine])
+
+    routes_x = [route(p_sort, p_recv), route(x_sort, x_recv.at[place.z])]
+    load_c.wait()
+    c_sort[...] = pick(leave, c_own[...], TN)
+    routes_c = [route(c_sort, c_recv.at[place.z])]
+    g_z.start()
+
+    def arrive(routes):
+        for copies, own in routes:
+            own.wait()
+            for copy in copies:
+                copy.wait_recv()
+
+    def spread(received):
+        mine = received.at[place.z]
+        return [links.remote(mine, mine, device) for device, _, _ in column]
+
+    arrive(routes_x)
+    spread_x = spread(x_recv)
+    g_x.forward()
+    g_s.forward()
+    g_o.start()
+    arrive(routes_c)
+    spread_c = spread(c_recv)
+    g_x.share()
+    g_s.share()
+
+    for copy in spread_x:
+        copy.wait_recv()
+    settle = (p_recv[:, :1] == iota((tok, tok), 1).astype(F32)).astype(BF16)
+    squares = jnp.zeros((tok, 1), F32)
+    for k in range(place.tp):
+        value = pick(settle, x_recv[k], TN)
+        tokens[k] = value
+        squares = squares + jnp.sum(value * value, axis=1, keepdims=True)
+    scale = lax.rsqrt(squares / (place.tp * slice_width) + EPSILON)
+    for k in range(place.tp):
+        high, low = split2(tokens[k] * scale * gain[:, k * slice_width : (k + 1) * slice_width])
+        n_high[k] = high
+        n_low[k] = low
+    stores = []
+    for k in range(place.tp):
+        stores.append(links.move(tokens.at[k], tokens_out.at[:, k * slice_width : (k + 1) * slice_width]))
+
+    g_z.forward()
+    g_x.finish()
+    g_s.finish()
+    stores += [links.move(wx, wx_out), links.move(ws, ws_out)]
+    project(n_high, n_low, wx, pre_x, 256)
+    project(n_high, n_low, ws, pre_s, 128)
+    g_z.share()
+    g_o.forward()
+    g_z.finish()
+    stores += [links.move(wz, wz_out)]
+    project(n_high, n_low, wz, gate_pre, 256)
+
+    for copy in spread_c:
+        copy.wait_recv()
+    for k in range(place.tp):
+        upstream[k] = pick(settle, c_recv[k], TN)
+        stores.append(links.move(upstream.at[k], upstream_out.at[:, k * slice_width : (k + 1) * slice_width]))
+    for k in range(place.tp):
+        high, low = split2(upstream[k])
+        n_high[k] = high
+        n_low[k] = low
+    g_o.share()
+    g_o.finish()
+    stores += [links.move(wo, wo_out)]
+    project(n_high, n_low, wo, d_normal, 256)
+    for store in stores:
+        store.wait()
+    links.finish()
+
+
+def forward_call(sizes, slots, gain_in, inputs, cotangent, w_x, w_s, w_z, w_out):
+    fsdp, _, tp = sizes
+    tok, width = inputs.shape
+    shard, inner = w_x.shape
+    side = w_s.shape[1]
+    depth = shard * 2 * fsdp
+    part = width // tp
+    grid_side = math.isqrt(fsdp)
+    copies = 4 * gather_copies(grid_side) + 3 * (2 * fsdp - 1) + 2 * (tp - 1)
+    anywhere = pl.BlockSpec(memory_space=pl.ANY)
+    inside = pl.BlockSpec(memory_space=pltpu.VMEM)
+
+    def shape(*dims):
+        return jax.ShapeDtypeStruct(dims, F32)
+
+    return pl.pallas_call(
+        functools.partial(forward_kernel, sizes),
+        out_shape=(
+            shape(tok, width),
+            shape(tok, width),
+            shape(tok, 128),
+            shape(tok, inner),
+            shape(tok, side),
+            shape(tok, inner),
+            shape(tok, inner),
+            shape(depth, inner),
+            shape(depth, side),
+            shape(depth, inner),
+            shape(depth, inner),
+        ),
+        in_specs=[inside, inside] + [anywhere] * 6,
+        out_specs=(anywhere, anywhere, inside, inside, inside, inside, inside, anywhere, anywhere, anywhere, anywhere),
+        scratch_shapes=[
+            pltpu.VMEM((depth, inner), F32),
+            pltpu.VMEM((depth, side), F32),
+            pltpu.VMEM((depth, inner), F32),
+            pltpu.VMEM((depth, inner), F32),
+            pltpu.VMEM((tok, part), F32),
+            pltpu.VMEM((tok, part), F32),
+            pltpu.VMEM((tok, part), F32),
+            pltpu.VMEM((tok, part), F32),
+            pltpu.VMEM((tok, 128), F32),
+            pltpu.VMEM((tp, tok, part), F32),
+            pltpu.VMEM((tp, tok, part), F32),
+            pltpu.VMEM((tp, tok, part), F32),
+            pltpu.VMEM((tp, tok, part), F32),
+            pltpu.VMEM((tp, tok, part), BF16),
+            pltpu.VMEM((tp, tok, part), BF16),
+            pltpu.SemaphoreType.DMA((copies,)),
+            pltpu.SemaphoreType.DMA((copies,)),
+            pltpu.SemaphoreType.DMA((2 + 3 + 4 + 2 * tp + 4,)),
+        ],
+        compiler_params=pltpu.CompilerParams(collective_id=0, has_side_effects=True, vmem_limit_bytes=VMEM_LIMIT),
+        name="gather_project",
+    )(slots, gain_in, inputs, cotangent, w_x, w_s, w_z, w_out)
+
+
+HIGH = lax.Precision.HIGH
 
 
 def passed_along(block, axis, distance):
@@ -155,50 +565,15 @@
     ranks = jnp.sum((jnp.cumsum(onehot, axis=0) - onehot) * onehot, axis=1)
     send_at = targets * per_pair + ranks
     places = slots - targets * tok_count
-    x_send = jnp.zeros((groups * per_pair, model_width), jnp.float32).at[send_at].set(inputs)
-    c_send = jnp.zeros((groups * per_pair, model_width), jnp.float32).at[send_at].set(cotangent)
-    p_send = jnp.full((groups * per_pair,), tok_count, jnp.int32).at[send_at].set(places)
-    x_recv, c_recv, p_recv = (
-        lax.all_to_all(
-            x_send.reshape(groups, per_pair, model_width),
-            ("fsdp", "ctx"),
-            split_axis=0,
-            concat_axis=0,
-            tiled=True,
-        ),
-        lax.all_to_all(
-            c_send.reshape(groups, per_pair, model_width),
-            ("fsdp", "ctx"),
-            split_axis=0,
-            concat_axis=0,
-            tiled=True,
-        ),
-        lax.all_to_all(
-            p_send.reshape(groups, per_pair),
-            ("fsdp", "ctx"),
-            split_axis=0,
-            concat_axis=0,
-            tiled=True,
-        ),
-    )
-    p_flat = p_recv.reshape(-1)
-    tokens = (
-        jnp.zeros((tok_count, model_width), jnp.float32)
-        .at[p_flat]
-        .set(x_recv.reshape(-1, model_width), mode="drop")
-    )
-    upstream = (
-        jnp.zeros((tok_count, model_width), jnp.float32)
-        .at[p_flat]
-        .set(c_recv.reshape(-1, model_width), mode="drop")
-    )
-    gate_w, chan_w, step_w, state_w, proj_w = (
-        lax.all_gather(w_z, ("fsdp", "ctx"), axis=0, tiled=True),
-        lax.all_gather(w_x, ("fsdp", "ctx"), axis=0, tiled=True),
-        lax.all_gather(w_dt, ("fsdp", "ctx"), axis=0, tiled=True),
-        lax.all_gather(w_bc, ("fsdp", "ctx"), axis=0, tiled=True),
-        lax.all_gather(w_out, ("fsdp", "ctx"), axis=0, tiled=True),
-    )
+    lead = (lax.axis_size("fsdp"), lax.axis_size("ctx"), tp_count)
+    heads = w_dt.shape[1]
+    w_side = jnp.concatenate([w_bc, w_dt, jnp.zeros((w_dt.shape[0], 128 - heads), jnp.float32)], axis=1)
+    slots_wide = jnp.broadcast_to(slots[:, None], (tok_count, 128))
+    tokens, upstream, p_recv, pre_x, pre_s, gate_pre, d_normal, chan_w, side_w, gate_w, proj_w = forward_call(
+        lead, slots_wide, gain_in[None, :], inputs, cotangent, w_x, w_side, w_z, w_out
+    )
+    state_w, step_w = side_w[:, : 2 * N], side_w[:, 2 * N : 2 * N + heads]
+    p_flat = p_recv[:, 0].astype(jnp.int32)
     inner_local = gate_w.shape[1]
     lengths = seq_lengths[0]
     offset = lax.axis_index("ctx") * tok_count
@@ -207,9 +582,8 @@
     tail_segs = segment_of(offset - width + 1 + jnp.arange(width - 1, dtype=jnp.int32), lengths)
     seg_before = segment_of(jnp.reshape(offset - 1, (1,)), lengths)[0]
     normed, norm_back = jax.vjp(norm_in, tokens, gain_in)
-    gate_pre = matmul(normed, gate_w)
-    pre = jnp.concatenate([matmul(normed, chan_w), matmul(normed, state_w)], axis=1)
-    raw_dt = matmul(normed, step_w)
+    pre = jnp.concatenate([pre_x, pre_s[:, : 2 * N]], axis=1)
+    raw_dt = pre_s[:, 2 * N : 2 * N + heads]
     tail = passed_along(pre[tok_count - width + 1 :], "ctx", 1)
     taps = jnp.concatenate([conv_x, conv_bc], axis=1)
     bias = jnp.concatenate([conv_x_bias, conv_bc_bias])
@@ -247,7 +621,6 @@
     own_cols = lax.dynamic_slice_in_dim(tokens, tp_index * slice_width, slice_width, 1)
     result_rows = own_cols + branch_out
     g_out = matmul_tn(upstream, normal_y)
-    d_normal = matmul(upstream, proj_w)
     g_gate_gain = jnp.sum(d_normal * gated * gscale[:, None], axis=0)
     inner_part = jnp.sum(d_normal * gate_gain[None, :] * gated, axis=1)
     inner_total = lax.psum(inner_part, "tp")

time: 790 us -> 756 us (0.957)
  Pallas kernels: 0 us -> 144 us
  matrix products: 162 us -> 92.3 us
  waiting for transfers between devices: 360 us -> 310 us
  blocking collectives: 86.3 us -> 59.6 us
  starting transfers between devices: 40.4 us -> 16.9 us
  local copies, waits for them, and re-layouts: 64.1 us -> 53.6 us
    pallas_call x0 -> x1, Pallas kernels: none -> 144 us  [forward_call(): pl.pallas_call(functools.partial(forward_kernel, sizes), out_shape=(shape...]
    all_gather x4 -> x0, waiting for transfers between devices: 69.3 us -> none  [the longest x1 37.7 us: shards(): lax.all_gather(w_x, ('fsdp', 'ctx'), axis=0, tiled=True)]
    dot_general x5 -> x0, matrix products: 38.6 us -> none  [matmul(): return jnp.dot(left, right, precision=HIGH)]
    all_gather x1 -> x0, blocking collectives: 28.7 us -> none  [shards(): lax.all_gather(w_dt, ('fsdp', 'ctx'), axis=0, tiled=True)]
    scatter x5 -> x0, local copies, waits for them, and re-layouts: 18.1 us -> none  [the longest x2 8.74 us: shards(): jnp.zeros((groups * per_pair, model_width), jnp.float32).at[send_at]]
    reduce_scatter x1, waiting for transfers between devices: 18.5 us -> 33.1 us  [shards(): lax.psum_scatter(d_tokens_part, 'tp', scatter_dimension=1, tiled=True)]
    all_to_all x3 -> x0, starting transfers between devices: 13.7 us -> none  [the longest x1 5.17 us: shards(): lax.all_to_all(p_send.reshape(groups, per_pair), ('fsdp', 'ctx'), split_a...]
    dot_general x5, matrix products: 35.7 us -> 23.8 us  [matmul_tn(): lax.dot_general(left, right, (((0,), (0,)), ((), ())), precision=HIGH)]
  transfers between devices with their start and end apart: 21 -> 14, of which waited for: 9 -> 7; matrix products, arithmetic and copies ran while one was open for 24% -> 13% of each run, Pallas kernels for 0% -> 0%
where the time goes in v1:
time: 756 us; the launch traced here: 746 us
  waiting for transfers between devices  310 us (41%)
  Pallas kernels  144 us (19%)
  matrix products  92.3 us (12%)
  blocking collectives  59.6 us (8%)
  local copies, waits for them, and re-layouts  53.6 us (7%)
  other arithmetic  51.5 us (7%)
  between operations  19 us (3%)
  starting transfers between devices  16.9 us (2%)
    pallas_call x1, Pallas kernels, forward_call(): pl.pallas_call(functools.partial(forward_kernel, sizes), out_shape=(shape...  144 us
    reduce_scatter x1, waiting for transfers between devices, shards(): lax.psum_scatter(g_chan_w, ('fsdp', 'ctx'), scatter_dimension=0, tiled=True)  75.8 us
    reduce_scatter x1, waiting for transfers between devices, shards(): lax.psum_scatter(g_gate_w, ('fsdp', 'ctx'), scatter_dimension=0, tiled=True)  75.6 us
    reduce_scatter x1, waiting for transfers between devices, shards(): lax.psum_scatter(g_out, ('fsdp', 'ctx'), scatter_dimension=0, tiled=True)  75.3 us
    reduce_scatter x1, waiting for transfers between devices, shards(): lax.psum_scatter(g_state_w, ('fsdp', 'ctx'), scatter_dimension=0, tiled=T...  36.5 us
    dot_general x9, matrix products, matmul_nt(): lax.dot_general(left, right, (((1,), (1,)), ((), ())), precision=HIGH)  33.6 us
    reduce_scatter x1, waiting for transfers between devices, shards(): lax.psum_scatter(d_tokens_part, 'tp', scatter_dimension=1, tiled=True)  33.1 us
    psum x1, blocking collectives, shards(): lax.psum((g_taps[:, :inner_local], g_bias[:inner_local], g_taps[:, inner_...  23.9 us
  transfers between devices with their start and end apart: 14, of which 7 were waited for; matrix products, arithmetic and copies ran while one was open for 13% of the time, Pallas kernels for 0%

profile of v1, /device:TPU:0, one launch (start us, length us, event | category | flops | bytes accessed | tf_op | source)
XLA Modules:
  0.0 746.4 jit_solution(9176502630041907363)
XLA Ops:
  11.3 143.8 %gather_project.1 = (f32[256,2048]{1,0:T(8,128)}, f32[256,2048]{1,0:T(8,128)}, f32[256,128]{1,0:T(8,128)}, f32[256,1024]{1,0:T(8,128)}, f32[256,384]{1,0:T(8,128...) custom-call(s32[256,128]{1,0:T(8,128)} %broadcast_in_dim.184.slots_i, ...), custom_call_target="tpu_custom_call" | custom-call | tf_op jit(solution)/shard_map/gather_project/pallas_call | solution.py:380
  157.7 4.2 collective-permute-start
  165.9 1.9 compare_convert_fusion.3
  174.5 3.3 fusion.44
  180.1 2.5 copy.161
  182.7 1.9 convolution_add_fusion.3
  188.1 3.0 fusion.27
  192.7 2.7 multiply_add_fusion.1
  195.4 2.5 copy.164
  198.0 2.8 multiply_reduce_fusion.14
  200.8 17.2 %psum.91 = f32[256]{0:T(256)S(1)} all-reduce(f32[256]{0:T(256)S(1)} %get-tuple-element.282), channel_id=1, replica_groups=mesh['fsdp'=4,'ctx'=2,'tp'=4] {'tp'}, use_global_device_ids=true, to_apply=%region_7.8 | all-reduce | flops 256 | bytes 2048 | tf_op jit(solution)/shard_map/psum | solution.py:615
  218.0 2.4 multiply_reduce_fusion.10
  220.4 8.3 %psum.92 = f32[256]{0:T(256)S(1)} all-reduce(f32[256]{0:T(256)S(1)} %get-tuple-element.257), channel_id=1, replica_groups=mesh['fsdp'=4,'ctx'=2,'tp'=4] {'tp'}, use_global_device_ids=true, to_apply=%region_13.14 | all-reduce | flops 256 | bytes 2048 | tf_op jit(solution)/shard_map/psum | solution.py:626
  228.8 4.1 fusion.77
  232.9 2.5 copy.166
  237.3 2.3 fusion.71
  244.2 2.5 reduce-window.72
  247.7 3.0 convolution_bitcast_fusion.1
  255.3 2.5 copy.170
  265.1 2.1 fusion.45
  269.0 3.2 multiply_reduce_fusion.11
  272.4 5.9 fusion.13
  285.9 2.0 fusion.99
  288.9 2.5 reduce-window.70
  293.1 2.7 fusion.94
  297.7 3.2 fusion.48
  300.9 2.6 fusion.47
  303.8 8.7 %fusion.63 = f32[256,2048]{1,0:T(8,128)} fusion(f32[2048,1024]{1,0:T(8,128)} %get-tuple-element.227, f32[256,1024]{1,0:T(8,128)} %get-tuple-element.283, f32[256]{0:T(256)S(1)} %add_rsqrt_fusion, f32[1024]{0:T(1024)S(1)} %copy-done.32), kind=kOutput, calls=%fused_computation.100 | convolution fusion | flops 3221749760 | bytes 11539456 | tf_op jit(solution)/shard_map/dot_general | solution.py:436
  312.6 8.8 %fusion.133 = f32[256,2048]{1,0:T(8,128)} fusion(f32[256,1024]{1,0:T(8,128)} %get-tuple-element.289, f32[2048,1024]{1,0:T(8,128)} %get-tuple-element.231), kind=kOutput, calls=%fused_computation.252 | convolution fusion | flops 3221225472 | bytes 11534336 | tf_op jit(solution)/shard_map/dot_general | solution.py:436
  321.5 3.4 fusion.39
  324.9 2.6 copy.175
  327.4 12.0 %all-reduce.20.cloned.1.call-done = (f32[256,128]{1,0:T(8,128)}, f32[256,128]{1,0:T(8,128)}) async-done(((f32[256,128]{1,0:T(8,128)}, f32[256,128]{1,0:T(8,128)}), (f32[256,128]{1,0:T(8,128)}, f32[256,128]{1,0:T(8,128)})) %all-reduce.20.cloned.1.call-update) | async-done | bytes 262160 | tf_op jit(solution)/shard_map/psum | solution.py:637
  339.5 3.4 multiply_reduce_fusion.7
  346.8 8.3 %convolution_add_fusion.2 = f32[256,2048]{1,0:T(8,128)S(1)} fusion(f32[256,2048]{1,0:T(8,128)} %fusion.133, f32[2048,1024]{1,0:T(8,128)} %get-tuple-element.245, f32[256,1280]{1,0:T(8,128)S(1)} %scatter-add.4), kind=kOutput, calls=%fused_computation.22 | convolution fusion | flops 3221749760 | bytes 13631488 | tf_op jit(solution)/shard_map/dot_general | solution.py:436
  356.2 2.4 multiply_reduce_fusion.2
  361.9 3.2 fusion.35
  366.4 5.9 fusion.38
  373.5 7.4 fusion.49
  382.3 5.8 fusion.37
  392.8 3.8 all-to-all-start
  397.9 33.1 %reduce-scatter.10.cloned.1.call-done = f32[256,512]{1,0:T(8,128)} async-done(((f32[256,2048]{1,0:T(8,128)}), f32[256,512]{1,0:T(8,128)}) %reduce-scatter.10.cloned.1.call-update) | async-done | bytes 524304 | tf_op jit(solution)/shard_map/reduce_scatter | solution.py:658
  434.3 3.7 all-to-all-start.1
  438.2 10.2 %all-reduce.15 = f32[2048]{0:T(1024)S(1)} all-reduce(f32[2048]{0:T(1024)S(1)} %copy-done.41), channel_id=9, replica_groups=mesh['fsdp'=4,'ctx'=2,'tp'=4] {'tp'}, use_global_device_ids=true, to_apply=%region_57.58.clone | all-reduce | flops 2048 | bytes 16384
  448.5 23.9 %all-reduce.16 = (f32[4,1024]{1,0:T(4,128)}, f32[1024]{0:T(1024)}, f32[4,256]{1,0:T(4,128)}, f32[256]{0:T(256)}, f32[16]{0:T(128)}, /*index=5*/f32[16]{0:T(128)}, f32[16]{0:T(128)}, f32[1024]{0:T(1024)}, f32[512]{0:T(512)}) all-reduce(f32[4,1024]{1,0:T(4,128)S(1)} %slice.233, ...), channel_id=1, replica_groups=mesh['fsdp'=4,'ctx'=2,'tp'=4] {'fsdp','ctx'}, use_global_device_ids=true, to_apply=%region_42.43 | all-reduce | flops 7984 | bytes 63872 | tf_op jit(solution)/shard_map/psum | solution.py:691
  475.9 36.5 %reduce-scatter.18.cloned.1.call-done = f32[256,256]{1,0:T(8,128)} async-done(((f32[2048,256]{1,0:T(8,128)}), f32[256,256]{1,0:T(8,128)}) %reduce-scatter.18.cloned.1.call-update) | async-done | bytes 262160 | tf_op jit(solution)/shard_map/reduce_scatter | solution.py:688
  512.4 75.6 %reduce-scatter.12.cloned.1.call-done = f32[256,1024]{1,0:T(8,128)} async-done(((f32[2048,1024]{1,0:T(8,128)}), f32[256,1024]{1,0:T(8,128)}) %reduce-scatter.12.cloned.1.call-update) | async-done | bytes 1048592 | tf_op jit(solution)/shard_map/reduce_scatter | solution.py:685
  588.0 75.3 %reduce-scatter.20.cloned.1.call-done = f32[256,1024]{1,0:T(8,128)} async-done(((f32[2048,1024]{1,0:T(8,128)}), f32[256,1024]{1,0:T(8,128)}) %reduce-scatter.20.cloned.1.call-update) | async-done | bytes 1048592 | tf_op jit(solution)/shard_map/reduce_scatter | solution.py:689
  663.3 75.8 %reduce-scatter.14.cloned.1.call-done = f32[256,1024]{1,0:T(8,128)} async-done(((f32[2048,1024]{1,0:T(8,128)}), f32[256,1024]{1,0:T(8,128)}) %reduce-scatter.14.cloned.1.call-update) | async-done | bytes 1048592 | tf_op jit(solution)/shard_map/reduce_scatter | solution.py:686
  (317 shorter events, 79.6 us)
Async XLA Ops:
  7.2 332.3 %all-reduce.20.cloned.1.call-start = ((), (), s32[]{:S(2)}) async-start(), calls=%async_computation.16 | async-start | bytes 524288 | tf_op jit(solution)/shard_map/psum | solution.py:637
  11.3 150.7 %copy-start.53 = (f32[4,1024]{1,0:T(4,128)S(1)}, f32[4,1024]{1,0:T(4,128)}, u32[]{:S(2)}) copy-start(f32[4,1024]{1,0:T(4,128)} %param.30) | copy-start | bytes 49156
  11.3 150.7 %copy-start.62 = (f32[4,256]{1,0:T(4,128)S(1)}, f32[4,256]{1,0:T(4,128)}, u32[]{:S(2)}) copy-start(f32[4,256]{1,0:T(4,128)} %param.32) | copy-start | bytes 12292
  11.3 150.8 %copy-start.76 = (s32[1,4]{1,0:T(1,128)S(1)}, s32[1,4]{1,0:T(1,128)}, u32[]{:S(2)}) copy-start(s32[1,4]{1,0:T(1,128)} %param.22) | copy-start | bytes 52
  11.3 156.5 %copy-start.74 = (f32[16]{0:T(128)S(1)}, f32[16]{0:T(128)}, u32[]{:S(2)}) copy-start(f32[16]{0:T(128)} %param.35) | copy-start | bytes 196
  11.3 156.6 %copy-start.64 = (f32[16]{0:T(128)S(1)}, f32[16]{0:T(128)}, u32[]{:S(2)}) copy-start(f32[16]{0:T(128)} %param.34) | copy-start | bytes 196
  155.1 15.5 %copy-start = (f32[256,2048]{1,0:T(8,128)S(1)}, f32[256,2048]{1,0:T(8,128)}, u32[]{:S(2)}) copy-start(f32[256,2048]{1,0:T(8,128)} %get-tuple-element.223) | copy-start | bytes 6291460
  157.7 13.8 %copy-start.63 = (f32[1024]{0:T(1024)S(1)}, f32[1024]{0:T(1024)}, u32[]{:S(2)}) copy-start(f32[1024]{0:T(1024)} %param.31) | copy-start | bytes 12292
  157.7 13.8 %copy-start.70 = (f32[256]{0:T(256)S(1)}, f32[256]{0:T(256)}, u32[]{:S(2)}) copy-start(f32[256]{0:T(256)} %param.33) | copy-start | bytes 3076
  157.7 15.3 %collective-permute-start = (f32[3,1280]{1,0:T(4,128)S(1)}, f32[3,1280]{1,0:T(4,128)S(1)}, u32[]{:S(2)}, u32[]{:S(2)}) collective-permute-start(f32[3,1280]{1,0:T(4,128)S(1)} %fusion.109), channel_id=1, source_target_pairs={{0,4},{1,5},{2,6},{3,7},{8,12},{9,13},{10,14},{11,15},{16,20},{17,... | collective-permute-start | bytes 46088 | tf_op jit(solution)/shard_map/ppermute | solution.py:428
  167.8 6.6 copy-start.54
  180.1 7.9 %copy-start.51 = (f32[16,256]{1,0:T(8,128)S(1)}, f32[16,256]{1,0:T(8,128)}, u32[]{:S(2)}) copy-start(f32[16,256]{1,0:T(8,128)} %copy.158) | copy-start | bytes 49156
  184.6 6.4 collective-permute-start.1
  197.9 20.1 %copy-start.32 = (f32[1024]{0:T(1024)S(1)}, f32[1024]{0:T(1024)}, u32[]{:S(2)}) copy-start(f32[1024]{0:T(1024)} %param.37) | copy-start | bytes 12292
  218.0 85.8 %copy-start.42 = (f32[256]{0:T(256)}, f32[256]{0:T(256)S(1)}, u32[]{:S(2)}) copy-start(f32[256]{0:T(256)S(1)} %add_rsqrt_fusion) | copy-start | bytes 3076
  239.5 11.1 %collective-permute-start.2 = (f32[16,64,128]{2,1,0:T(8,128)}, f32[16,64,128]{2,1,0:T(8,128)}, u32[]{:S(2)}, u32[]{:S(2)}) collective-permute-start(f32[16,64,128]{2,1,0:T(8,128)} %fusion.71), channel_id=1, source_target_pairs={{4,0},{5,1},{6,2},{7,3},{12,8},{13,9},{14,10},{15,11},{20,16},{21,... | collective-permute-start | bytes 1572872 | tf_op jit(solution)/shard_map/ppermute | solution.py:428
  265.0 7.4 copy-start.28
  265.1 7.2 copy-start.13
  272.3 6.0 copy-start.33
  272.4 5.9 copy-start.21
  281.8 10.6 %copy-start.50 = (f32[16,256]{1,0:T(8,128)S(1)}, f32[16,256]{1,0:T(8,128)}, u32[]{:S(2)}) copy-start(f32[16,256]{1,0:T(8,128)} %get-tuple-element.249) | copy-start | bytes 49156
  303.6 86.3 %reduce-scatter.8.cloned.1.call-start = ((), (), s32[]{:S(2)}) async-start(), calls=%async_computation.9 | async-start | bytes 2621440 | tf_op jit(solution)/shard_map/reduce_scatter | solution.py:618
  312.5 118.6 %reduce-scatter.10.cloned.1.call-start = ((), (), s32[]{:S(2)}) async-start(), calls=%async_computation.10 | async-start | bytes 2621440 | tf_op jit(solution)/shard_map/reduce_scatter | solution.py:658
  312.5 8.9 %copy-start.7 = (f32[256,1024]{0,1:T(8,128)S(1)}, f32[256,1024]{0,1:T(8,128)}, u32[]{:S(2)}) copy-start(f32[256,1024]{0,1:T(8,128)} %copy.170) | copy-start | bytes 3145732
  312.5 8.9 %copy-start.26 = (f32[256,16,64]{0,2,1:T(8,128)S(1)}, f32[256,16,64]{0,2,1:T(8,128)}, u32[]{:S(2)}) copy-start(f32[256,16,64]{0,2,1:T(8,128)} %get-tuple-element.313) | copy-start | bytes 3145732
  312.6 8.9 %copy-start.29 = (f32[256,256]{1,0:T(8,128)S(1)}, f32[256,256]{1,0:T(8,128)}, u32[]{:S(2)}) copy-start(f32[256,256]{1,0:T(8,128)} %copy-done.28) | copy-start | bytes 786436
  312.6 8.9 %copy-start.34 = (pred[256,256]{1,0:T(8,128)(4,1)S(1)}, pred[256,256]{1,0:T(8,128)(4,1)}, u32[]{:S(2)}) copy-start(pred[256,256]{1,0:T(8,128)(4,1)} %copy-done.33) | copy-start | bytes 196612
  312.6 8.9 %copy-start.47 = (f32[16,256]{1,0:T(8,128)S(1)}, f32[16,256]{1,0:T(8,128)}, u32[]{:S(2)}) copy-start(f32[16,256]{1,0:T(8,128)} %copy.173) | copy-start | bytes 49156
  312.6 8.9 %copy-start.49 = (f32[16,256]{1,0:T(8,128)S(1)}, f32[16,256]{1,0:T(8,128)}, u32[]{:S(2)}) copy-start(f32[16,256]{1,0:T(8,128)} %copy.171) | copy-start | bytes 49156
  312.6 8.9 %copy-start.73 = (f32[16]{0:T(128)S(1)}, f32[16]{0:T(128)}, u32[]{:S(2)}) copy-start(f32[16]{0:T(128)} %param.36) | copy-start | bytes 196
  324.8 14.6 %copy-start.55 = (f32[256]{0:T(256)S(1)}, f32[256]{0:T(256)}, u32[]{:S(2)}) copy-start(f32[256]{0:T(256)} %copy-done.54) | copy-start | bytes 3076
  324.9 14.6 %copy-start.56 = (f32[256]{0:T(256)S(1)}, f32[256]{0:T(256)}, u32[]{:S(2)}) copy-start(f32[256]{0:T(256)} %get-tuple-element.311) | copy-start | bytes 3076
  324.9 14.6 %copy-start.57 = (f32[256]{0:T(256)S(1)}, f32[256]{0:T(256)}, u32[]{:S(2)}) copy-start(f32[256]{0:T(256)} %get-tuple-element.312) | copy-start | bytes 3076
  343.4 3.1 collective-permute-start.3
  346.7 15.2 %copy-start.8 = (f32[256,1280]{1,0:T(8,128)}, f32[256,1280]{1,0:T(8,128)S(1)}, u32[]{:S(2)}) copy-start(f32[256,1280]{1,0:T(8,128)S(1)} %scatter-add.4) | copy-start | bytes 3932164
  346.8 8.3 %copy-start.18 = (f32[2048,384]{1,0:T(8,128)S(1)}, f32[2048,384]{1,0:T(8,128)}, u32[]{:S(2)}) copy-start(f32[2048,384]{1,0:T(8,128)} %get-tuple-element.246) | copy-start | bytes 9437188
  346.8 8.3 %copy-start.23 = (f32[256,16]{1,0:T(8,128)S(1)}, f32[256,16]{1,0:T(8,128)}, u32[]{:S(2)}) copy-start(f32[256,16]{1,0:T(8,128)} %get-tuple-element.297) | copy-start | bytes 49156
  360.4 115.5 %reduce-scatter.16.cloned.1.call-start = ((), (), s32[]{:S(2)}) async-start(), calls=%async_computation.13 | async-start | bytes 147456 | tf_op jit(solution)/shard_map/reduce_scatter | solution.py:687
  361.9 150.5 %reduce-scatter.18.cloned.1.call-start = ((), (), s32[]{:S(2)}) async-start(), calls=%async_computation.14 | async-start | bytes 2359296 | tf_op jit(solution)/shard_map/reduce_scatter | solution.py:688
  365.2 222.8 %reduce-scatter.12.cloned.1.call-start = ((), (), s32[]{:S(2)}) async-start(), calls=%async_computation.11 | async-start | bytes 9437184 | tf_op jit(solution)/shard_map/reduce_scatter | solution.py:685
  372.3 291.0 %reduce-scatter.20.cloned.1.call-start = ((), (), s32[]{:S(2)}) async-start(), calls=%async_computation.15 | async-start | bytes 9437184 | tf_op jit(solution)/shard_map/reduce_scatter | solution.py:689
  381.0 358.1 %reduce-scatter.14.cloned.1.call-start = ((), (), s32[]{:S(2)}) async-start(), calls=%async_computation.12 | async-start | bytes 9437184 | tf_op jit(solution)/shard_map/reduce_scatter | solution.py:686
  392.8 41.5 %all-to-all-start = ((f32[8,32,512]{2,1,0:T(8,128)}), f32[8,32,512]{2,1,0:T(8,128)S(1)}, u32[]{:S(2)}, u32[]{:S(2)}) async-start(f32[8,32,512]{2,1,0:T(8,128)} %bitcast.17), calls=%async_computation.1 | async-start | bytes 1048576 | tf_op jit(solution)/shard_map/all_to_all | solution.py:667
  432.5 5.7 copy-start.41
  432.5 16.0 %copy-start.44 = (f32[1024]{0:T(1024)S(1)}, f32[1024]{0:T(1024)}, u32[]{:S(2)}) copy-start(f32[1024]{0:T(1024)} %get-tuple-element.256) | copy-start | bytes 12292
  432.5 16.0 %copy-start.65 = (f32[16]{0:T(128)S(1)}, f32[16]{0:T(128)}, u32[]{:S(2)}) copy-start(f32[16]{0:T(128)} %get-tuple-element.260) | copy-start | bytes 196
  432.5 16.0 %copy-start.66 = (f32[16]{0:T(128)S(1)}, f32[16]{0:T(128)}, u32[]{:S(2)}) copy-start(f32[16]{0:T(128)} %get-tuple-element.296) | copy-start | bytes 196
  434.3 39.8 %all-to-all-start.1 = ((f32[8,32,512]{2,1,0:T(8,128)}), f32[8,32,512]{2,1,0:T(8,128)S(1)}, u32[]{:S(2)}, u32[]{:S(2)}) async-start(f32[8,32,512]{2,1,0:T(8,128)} %bitcast.53), calls=%async_computation.3 | async-start | bytes 1048576 | tf_op jit(solution)/shard_map/all_to_all | solution.py:674
  (44 other events, 156.9 us)
Sparse Core Ops, SparseCore 0:
  303.7 35.7 all-reduce.19
  341.9 43.6 reduce-scatter.7
  387.8 43.1 reduce-scatter.9
  434.8 32.6 reduce-scatter.15
  471.2 41.1 reduce-scatter.17
  516.7 71.2 reduce-scatter.11
  592.1 71.2 reduce-scatter.19
  667.8 71.2 reduce-scatter.13
